TPU v7x, 32 devices: a whole 2x2x4 slice. The times are simulated.
32 devices in a mesh: expert: 4 (over x, core), cuts: 8 (over z, y).
Axes of the slice: x: 2, y: 2, z: 4, core: 2. Of those that a mesh axis runs over, the one named last changes fastest.
Arguments:
- out_grad: bfloat16 [256, 3072], P(('expert', 'cuts')), may hold values from -6 to 6
- routes: int32 [256, 2], P(('expert', 'cuts')), may hold values from 0 to 3, all different within a row; in each aligned block of 8 rows (0 to 7, 8 to 15, ...) at most 8 rows name the same one
- gate_weight: float32 [256, 2], P(('expert', 'cuts')), may hold values from 0.1 to 1
- gate_proj: bfloat16 [4, 3072, 16384], P('expert', None, 'cuts'), may hold values from -0.109375 to 0.109375
- up_proj: bfloat16 [4, 3072, 16384], P('expert', None, 'cuts'), may hold values from -0.109375 to 0.109375
- down_proj: bfloat16 [4, 16384, 3072], P('expert', 'cuts'), may hold values from -0.046875 to 0.046875
- saved_gate: bfloat16 [4, 256, 16384], P('expert', None, 'cuts'), may hold values from -6 to 6
- saved_up: bfloat16 [4, 256, 16384], P('expert', None, 'cuts'), may hold values from -6 to 6
Outputs:
- input_grad: bfloat16 [256, 3072], P(('expert', 'cuts'))
Inputs may be any that keep to these rules, and one draw needn't show every extreme that they name: `routes`: each token names two different experts. Among the 8 tokens of one device no expert is named more than 8 times, and in some devices one expert is named exactly 8 times.
All inputs are finite; a program needn't handle non-finite values.
Results may differ from a plain program's by a relative error of at most 0.0057.
Values may be sent and summed in bfloat16 or wider, within the bound.
A program may use at most 128 MiB of HBM per device.

v0:
```python
import jax
import jax.numpy as jnp
from jax import lax
from jax.sharding import PartitionSpec as P


def rank_slots(flat_routes):
    count = flat_routes.shape[-1]
    positions = jnp.arange(count, dtype=jnp.int32)
    before = positions[:, None] < positions[None, :]
    matches = flat_routes[..., :, None] == flat_routes[..., None, :]
    return jnp.sum(jnp.logical_and(matches, before), axis=-2)


def expert_rows(grad_rows, gate_mat, up_mat, down_mat, pre_gate, pre_up):
    contract = (((1,), (1,)), ((), ()))
    hidden_grad = lax.dot_general(grad_rows, down_mat, contract, preferred_element_type=jnp.float32)
    gate_vals = pre_gate.astype(jnp.float32)
    up_vals = pre_up.astype(jnp.float32)
    sigmoid_gate = jax.nn.sigmoid(gate_vals)
    up_grad = (hidden_grad * gate_vals * sigmoid_gate).astype(jnp.bfloat16)
    gate_grad = (
        hidden_grad * up_vals * sigmoid_gate * (1.0 + gate_vals * (1.0 - sigmoid_gate))
    ).astype(jnp.bfloat16)
    partial_value = lax.dot_general(
        gate_grad, gate_mat, contract, preferred_element_type=jnp.float32
    )
    return partial_value + lax.dot_general(
        up_grad, up_mat, contract, preferred_element_type=jnp.float32
    )


def shards(out_grad, routes, gate_weight, gate_proj, up_proj, down_proj, saved_gate, saved_up):
    expert_count = lax.axis_size("expert")
    cut_count = lax.axis_size("cuts")
    tok_rows = out_grad.shape[0]
    feature_dim = out_grad.shape[1]
    slot_count = saved_gate.shape[1] // (expert_count * cut_count)
    flat_routes = routes.reshape(-1)
    slot_index = rank_slots(flat_routes[None, :])[0]
    own_spots = flat_routes * slot_count + slot_index
    routed = (gate_weight[:, :, None] * out_grad.astype(jnp.float32)[:, None, :]).astype(
        jnp.bfloat16
    )
    routed = routed.reshape(2 * tok_rows, feature_dim)
    places = jnp.arange(expert_count * slot_count, dtype=jnp.int32)
    placing = (places[:, None] == own_spots[None, :]).astype(jnp.bfloat16)
    outgoing = jnp.dot(placing, routed, preferred_element_type=jnp.float32).astype(jnp.bfloat16)
    outgoing = outgoing.reshape(expert_count, slot_count, feature_dim)
    arrived = lax.all_to_all(outgoing, "expert", split_axis=0, concat_axis=0, tiled=True)
    gathered = lax.all_gather(arrived, "cuts", axis=0, tiled=True).reshape(-1, feature_dim)
    gate_block = saved_gate[0]
    up_block = saved_up[0]
    own_rows = lax.psum_scatter(
        expert_rows(gathered, gate_proj[0], up_proj[0], down_proj[0], gate_block, up_block),
        "cuts",
        scatter_dimension=0,
        tiled=True,
    )
    own_rows = own_rows.reshape(expert_count, slot_count, feature_dim)
    returned = lax.all_to_all(own_rows, "expert", split_axis=0, concat_axis=0, tiled=True).reshape(
        -1, feature_dim
    )
    picked = returned[own_spots].reshape(tok_rows, 2, feature_dim)
    summed = jnp.sum(picked, axis=1)
    return summed.astype(jnp.bfloat16)


def solution(mesh):
    in_specs = (
        P(("expert", "cuts"), None),
        P(("expert", "cuts"), None),
        P(("expert", "cuts"), None),
        P("expert", None, "cuts"),
        P("expert", None, "cuts"),
        P("expert", "cuts", None),
        P("expert", None, "cuts"),
        P("expert", None, "cuts"),
    )
    out_specs = P(("expert", "cuts"), None)
    return jax.shard_map(shards, mesh=mesh, in_specs=in_specs, out_specs=out_specs, check_vma=False)
```

profile of v0, /device:TPU:0, one launch (start us, length us, event | category | flops | bytes accessed | tf_op | source)
XLA Modules:
  0.0 188.8 jit_solution(4068992621880748433)
XLA Ops:
  6.5 0.0 all-gather.2.cloned.1.call-start
  6.5 0.8 copy.18
  7.3 0.1 reshape.151
  7.4 0.1 convert_reduce_fusion
  7.5 0.9 mul.58
  8.3 0.1 mul.59
  8.5 0.8 copy.19
  9.2 0.1 mul.56
  9.3 0.2 fusion.9
  9.6 9.4 %all_to_all.10 = bf16[4,8,3072]{2,1,0:T(8,128)(2,1)} all-to-all(bf16[4,8,3072]{2,1,0:T(8,128)(2,1)S(1)} %fusion.9), channel_id=1, replica_groups=mesh['expert'=4,'cuts'=8] {'expert'}, dimensions={0} | all-to-all | bytes 393216 | tf_op jit(solution)/shard_map/all_to_all | solution.py:50
  19.0 0.0 all-gather.2.cloned.1.call-update
  19.0 0.0 copy-start.1
  19.1 0.0 reduce-scatter.2.cloned.1.call-start
  19.1 45.0 %all-gather.2.cloned.1.call-done = bf16[32,8,3072]{2,1,0:T(8,128)(2,1)} async-done(((bf16[4,8,3072]{2,1,0:T(8,128)(2,1)}), bf16[32,8,3072]{2,1,0:T(8,128)(2,1)}) %all-gather.2.cloned.1.call-update) | async-done | bytes 1572880 | tf_op jit(solution)/shard_map/all_gather | solution.py:51
  64.1 6.9 %fusion.4 = f32[256,2048]{1,0:T(8,128)S(1)} fusion(bf16[1,2048,3072]{2,1,0:T(8,128)(2,1)} %param.13, bf16[32,8,3072]{2,1,0:T(8,128)(2,1)} %all-gather.2.cloned.1.call-done), kind=kOutput, calls=%fused_computation.5 | convolution fusion | flops 3221225472 | bytes 16252928 | tf_op jit(solution)/shard_map/dot_general | solution.py:17
  71.0 0.0 copy-done.1
  71.0 0.0 copy-start.2
  71.0 10.0 %fusion = f32[256,3072]{1,0:T(8,128)} fusion(bf16[1,3072,2048]{2,1,0:T(8,128)(2,1)} %param.12, f32[256,2048]{1,0:T(8,128)S(1)} %fusion.4, bf16[1,256,2048]{2,1,0:T(8,128)(2,1)S(1)} %copy-done.1), kind=kOutput, calls=%fused_computation.1 | convolution fusion | flops 3224895488 | bytes 18874368 | tf_op jit(solution)/shard_map/dot_general | solution.py:28
  81.0 0.0 copy-done.2
  81.0 15.0 %fusion.6 = f32[256,3072]{1,0:T(8,128)} fusion(f32[256,3072]{1,0:T(8,128)} %fusion, bf16[1,3072,2048]{2,1,0:T(8,128)(2,1)} %param.11, f32[256,2048]{1,0:T(8,128)S(1)} %fusion.4, bf16[1,256,2048]{2,1,0:T(8,128)(2,1)S(1)} %copy-done.2, bf16[1,256,2048]{2,1,0:T(8,128)(2,1)S(1)} %copy-done.1), kind=kOutput, calls=%fused_computation.7 | convolution fusion | flops 3228303360 | bytes 23068672 | tf_op jit(solution)/shard_map/dot_general | solution.py:25
  96.0 0.0 copy-start
  96.0 0.0 reduce-scatter.2.cloned.1.call-update
  96.0 0.7 copy-done
  96.7 0.1 copy.20
  96.8 0.1 mul.68
  96.9 72.6 %reduce-scatter.2.cloned.1.call-done = f32[32,3072]{1,0:T(8,128)} async-done(((f32[256,3072]{1,0:T(8,128)}), f32[32,3072]{1,0:T(8,128)}) %reduce-scatter.2.cloned.1.call-update) | async-done | bytes 393232 | tf_op jit(solution)/shard_map/reduce_scatter | solution.py:54
  169.5 3.5 %all-to-all-start.1 = ((f32[4,8,3072]{2,1,0:T(8,128)}), f32[4,8,3072]{2,1,0:T(8,128)S(1)}, u32[]{:S(2)}, u32[]{:S(2)}) async-start(f32[4,8,3072]{2,1,0:T(8,128)} %bitcast.41), calls=%async_computation.2 | async-start | bytes 786432 | tf_op jit(solution)/shard_map/all_to_all | solution.py:61
  173.0 7.4 %all-to-all-done.1 = f32[4,8,3072]{2,1,0:T(8,128)S(1)} async-done(((f32[4,8,3072]{2,1,0:T(8,128)}), f32[4,8,3072]{2,1,0:T(8,128)S(1)}, u32[]{:S(2)}, u32[]{:S(2)}) %all-to-all-start.1) | async-done | bytes 393248 | tf_op jit(solution)/shard_map/all_to_all | solution.py:61
  180.3 0.6 gather_fusion
  181.0 0.1 reshape.156
  181.1 0.9 reduce_sum.22
  (4 shorter events, 0.0 us)
Async XLA Ops:
  6.5 57.6 %all-gather.2.cloned.1.call-start = ((), (), s32[]{:S(2)}) async-start(), calls=%async_computation.3 | async-start | bytes 1769472 | tf_op jit(solution)/shard_map/all_gather | solution.py:51
  19.0 52.0 %copy-start.1 = (bf16[1,256,2048]{2,1,0:T(8,128)(2,1)S(1)}, bf16[1,256,2048]{2,1,0:T(8,128)(2,1)}, u32[]{:S(2)}) copy-start(bf16[1,256,2048]{2,1,0:T(8,128)(2,1)} %param.14) | copy-start | bytes 3145732
  19.1 150.4 %reduce-scatter.2.cloned.1.call-start = ((), (), s32[]{:S(2)}) async-start(), calls=%async_computation.4 | async-start | bytes 3538944 | tf_op jit(solution)/shard_map/reduce_scatter | solution.py:54
  71.0 10.0 %copy-start.2 = (bf16[1,256,2048]{2,1,0:T(8,128)(2,1)S(1)}, bf16[1,256,2048]{2,1,0:T(8,128)(2,1)}, u32[]{:S(2)}) copy-start(bf16[1,256,2048]{2,1,0:T(8,128)(2,1)} %param.15) | copy-start | bytes 3145732
  96.0 0.7 copy-start
  169.5 10.9 %all-to-all-start.1 = ((f32[4,8,3072]{2,1,0:T(8,128)}), f32[4,8,3072]{2,1,0:T(8,128)S(1)}, u32[]{:S(2)}, u32[]{:S(2)}) async-start(f32[4,8,3072]{2,1,0:T(8,128)} %bitcast.41), calls=%async_computation.2 | async-start | bytes 786432 | tf_op jit(solution)/shard_map/all_to_all | solution.py:61
Sparse Core Ops, SparseCore 0:
  19.2 44.8 all-gather.1
  96.2 73.2 reduce-scatter.1
where the time goes:
time: 189 us
  waiting for transfers between devices  125 us (66%)
  matrix products  32.1 us (17%)
  between operations  13.5 us (7%)
  blocking collectives  9.45 us (5%)
  local copies, waits for them, and re-layouts  4.23 us (2%)
  starting transfers between devices  3.5 us (2%)
    reduce_scatter x1, waiting for transfers between devices, shards(): lax.psum_scatter(expert_rows(gathered, gate_proj[0], up_proj[0], down_pro...  72.6 us
    all_gather x1, waiting for transfers between devices, shards(): lax.all_gather(arrived, 'cuts', axis=0, tiled=True).reshape(-1, feature_dim)  45 us
    dot_general x1, matrix products, expert_rows(): lax.dot_general(gate_grad, gate_mat, contract, preferred_element_type=jnp...  15 us
    dot_general x1, matrix products, expert_rows(): lax.dot_general(up_grad, up_mat, contract, preferred_element_type=jnp.flo...  10 us
    all_to_all x1, blocking collectives, shards(): lax.all_to_all(outgoing, 'expert', split_axis=0, concat_axis=0, tiled=True)  9.45 us
    all_to_all x1, waiting for transfers between devices, shards(): lax.all_to_all(own_rows, 'expert', split_axis=0, concat_axis=0, tiled=True)  7.38 us
    dot_general x1, matrix products, expert_rows(): lax.dot_general(grad_rows, down_mat, contract, preferred_element_type=jnp...  6.9 us
  transfers between devices with their start and end apart: 3, of which 3 were waited for; matrix products, arithmetic and copies ran while one was open for 0% of the time, Pallas kernels for 0%

commit v1 on v0

--- a/solution.py
+++ b/solution.py
@@ -1,7 +1,320 @@
 import jax
 import jax.numpy as jnp
 from jax import lax
+from jax.experimental import pallas as pl
+from jax.experimental.pallas import tpu as pltpu
 from jax.sharding import PartitionSpec as P
+
+MESH = pl.DeviceIdType.MESH
+TRANSPOSED = (((1,), (1,)), ((), ()))
+META = 128
+CHUNK = 512
+
+
+def fused_kernel(
+    tok, routes, gates, gate_hbm, up_hbm, down_hbm, sgate_hbm, sup_hbm, out,
+    gate_v, up_v, down_v, sgate_v, sup_v, blocks, rows, gate_g, up_g,
+    own, a_send, a_recv, col, b_send, b_recv, c_send, c_recv,
+    w_sem, s_sem, gs_sem, gr_sem, as_sem, ar_sem, bs_sem, br_sem, cs_sem, cr_sem,
+):
+    expert = lax.axis_index("expert")
+    cut = lax.axis_index("cuts")
+    x, core = expert // 2, expert % 2
+    z, y = cut // 2, cut % 2
+    feature = tok.shape[1]
+    half = feature // 2
+    hidden = down_v.shape[0]
+    total = rows.shape[0]
+    steps = feature // CHUNK
+    hidden_steps = hidden // CHUNK
+
+    column = [
+        None,
+        (expert, z * 2 + (1 - y)),
+        ((1 - x) * 2 + core, cut),
+        ((1 - x) * 2 + core, z * 2 + (1 - y)),
+    ]
+    depth = [None] + [(expert, ((z + d) % 4) * 2 + y) for d in (1, 2, 3)]
+    twin = (x * 2 + (1 - core), cut)
+
+    def down_copy(n):
+        part = pl.ds(pl.multiple_of(n * CHUNK, CHUNK), CHUNK)
+        return pltpu.make_async_copy(down_hbm.at[0, part], down_v.at[part], w_sem.at[0, n])
+
+    def gate_copy(n):
+        part = pl.ds(pl.multiple_of(n * CHUNK, CHUNK), CHUNK)
+        return pltpu.make_async_copy(gate_hbm.at[0, part], gate_v.at[part], w_sem.at[1, n])
+
+    def up_copy(n):
+        part = pl.ds(pl.multiple_of(n * CHUNK, CHUNK), CHUNK)
+        return pltpu.make_async_copy(up_hbm.at[0, part], up_v.at[part], w_sem.at[2, n])
+
+    saved = [
+        pltpu.make_async_copy(sgate_hbm.at[0], sgate_v, s_sem.at[0]),
+        pltpu.make_async_copy(sup_hbm.at[0], sup_v, s_sem.at[1]),
+    ]
+
+    barrier = pltpu.get_barrier_semaphore()
+    for peer in column[1:] + depth[1:] + [twin]:
+        pl.semaphore_signal(barrier, inc=1, device_id=peer, device_id_type=MESH)
+
+    for copy in saved:
+        copy.start()
+    for n in range(hidden_steps):
+        down_copy(n).start()
+    for n in range(steps):
+        gate_copy(n).start()
+        up_copy(n).start()
+
+    lane = lax.broadcasted_iota(jnp.int32, (8, META), 1)
+    level = lane // 32
+    name = lane % 32
+    first = (routes[:, 0:1] == name).astype(jnp.float32)
+    second = (routes[:, 1:2] == name).astype(jnp.float32)
+    hit = first + second
+    weight = first * gates[:, 0:1] + second * gates[:, 1:2]
+    sub = lax.broadcasted_iota(jnp.int32, (8, META), 0)
+    slot = jnp.zeros((8, META), jnp.float32)
+    for t in range(7):
+        slot = slot + jnp.where(sub > t, hit[t : t + 1, :], 0.0)
+    slot = jnp.where(hit > 0.0, slot, -1.0)
+    high = weight.astype(jnp.bfloat16).astype(jnp.float32)
+    middle = (weight - high).astype(jnp.bfloat16).astype(jnp.float32)
+    low = weight - high - middle
+    meta = jnp.where(
+        level == 0, high, jnp.where(level == 1, middle, jnp.where(level == 2, low, slot))
+    )
+    tokens = tok[...].astype(jnp.float32)
+    stacked = jnp.concatenate([tokens[:, :half], tokens[:, half:]], axis=0)
+    blocks[0, :, 0:half] = stacked.astype(jnp.bfloat16)
+    blocks[0, :, half : half + META] = jnp.concatenate(
+        [meta, jnp.zeros_like(meta)], axis=0
+    ).astype(jnp.bfloat16)
+
+    pl.semaphore_wait(barrier, 7)
+
+    def send(source, target, peer, sem):
+        copy = pltpu.make_async_remote_copy(
+            src_ref=blocks.at[source],
+            dst_ref=blocks.at[target],
+            send_sem=gs_sem.at[sem],
+            recv_sem=gr_sem.at[target],
+            device_id=peer,
+            device_id_type=MESH,
+        )
+        copy.start()
+        return copy
+
+    def arrived(index):
+        pltpu.make_async_remote_copy(
+            src_ref=blocks.at[index],
+            dst_ref=blocks.at[index],
+            send_sem=gs_sem.at[0],
+            recv_sem=gr_sem.at[index],
+            device_id=twin,
+            device_id_type=MESH,
+        ).wait_recv()
+
+    sent = []
+    for d in (1, 3, 2):
+        sent.append(send(0, 4 - d, depth[d], len(sent)))
+    for d in (0, 1, 3, 2):
+        if d:
+            arrived(d)
+        for g in (3, 1, 2):
+            sent.append(send(d, g * 4 + d, column[g], len(sent)))
+        sent.append(send(d, 16 + d, twin, len(sent)))
+    for d in (0, 1, 3, 2):
+        for g in (1, 2, 3):
+            arrived(g * 4 + d)
+            sent.append(send(g * 4 + d, 16 + g * 4 + d, twin, len(sent)))
+    for d in (0, 1, 3, 2):
+        for g in range(4):
+            arrived(16 + g * 4 + d)
+
+    info = blocks[:, :, half : half + META].astype(jnp.float32)[:, 0:8, :]
+    info = info.reshape(total, META)
+    lane = lax.broadcasted_iota(jnp.int32, (total, META), 1)
+    mine = (lane % 32) == expert
+    weight = jnp.sum(jnp.where(mine & (lane < 96), info, 0.0), axis=1, keepdims=True)
+    slot = jnp.sum(jnp.where(mine & (lane >= 96), info, 0.0), axis=1, keepdims=True)
+    place = lax.broadcasted_iota(jnp.int32, (total, total), 0)
+    far_core = (core + place // 128) % 2
+    far_x = (x + (place // 64) % 2) % 2
+    far_y = (y + (place // 32) % 2) % 2
+    far_z = (z + (place // 8) % 4) % 4
+    base = ((far_z * 2 + far_y) * 4 + far_x * 2 + far_core) * 8
+    spot = lax.broadcasted_iota(jnp.int32, (total, total), 1) - base
+    placing = (spot.astype(jnp.float32) == slot).astype(jnp.bfloat16)
+
+    quarter = half // 4
+    for n in range(4):
+        part = blocks[:, :, n * quarter : (n + 1) * quarter].astype(jnp.float32)
+        for h in range(2):
+            value = part[:, h * 8 : h * 8 + 8, :].reshape(total, quarter) * weight
+            start = h * half + n * quarter
+            rows[:, start : start + quarter] = value.astype(jnp.bfloat16)
+
+    for copy in saved:
+        copy.wait()
+
+    @pl.loop(0, hidden_steps)
+    def _(n):
+        down_copy(n).wait()
+        part = pl.ds(pl.multiple_of(n * CHUNK, CHUNK), CHUNK)
+        grad = lax.dot_general(
+            rows[...], down_v[part, :], TRANSPOSED, preferred_element_type=jnp.float32
+        )
+        a = jnp.dot(placing, sgate_v[:, part], preferred_element_type=jnp.float32)
+        b = jnp.dot(placing, sup_v[:, part], preferred_element_type=jnp.float32)
+        q = jax.nn.sigmoid(a)
+        up_g[:, part] = (grad * a * q).astype(jnp.bfloat16)
+        gate_g[:, part] = (grad * b * q * (1.0 + a * (1.0 - q))).astype(jnp.bfloat16)
+
+    def a_copy(j):
+        return pltpu.make_async_remote_copy(
+            src_ref=a_send.at[j],
+            dst_ref=a_recv.at[j],
+            send_sem=as_sem.at[j],
+            recv_sem=ar_sem.at[j],
+            device_id=twin,
+            device_id_type=MESH,
+        )
+
+    def b_copy(j, g):
+        return pltpu.make_async_remote_copy(
+            src_ref=b_send.at[j, g - 1],
+            dst_ref=b_recv.at[j, g - 1],
+            send_sem=bs_sem.at[j, g - 1],
+            recv_sem=br_sem.at[j, g - 1],
+            device_id=column[g],
+            device_id_type=MESH,
+        )
+
+    def c_copy(j, d):
+        return pltpu.make_async_remote_copy(
+            src_ref=c_send.at[j, d - 1],
+            dst_ref=c_recv.at[j, d - 1],
+            send_sem=cs_sem.at[j, d - 1],
+            recv_sem=cr_sem.at[j, d - 1],
+            device_id=depth[d],
+            device_id_type=MESH,
+        )
+
+    @pl.loop(0, steps + 3)
+    def _(i):
+        @pl.when(i < steps)
+        def _():
+            gate_copy(i).wait()
+            up_copy(i).wait()
+            part = pl.ds(pl.multiple_of(i * CHUNK, CHUNK), CHUNK)
+            value = lax.dot_general(
+                gate_g[...], gate_v[part, :], TRANSPOSED, preferred_element_type=jnp.float32
+            ) + lax.dot_general(
+                up_g[...], up_v[part, :], TRANSPOSED, preferred_element_type=jnp.float32
+            )
+            a_send[i] = value[128:256].astype(jnp.bfloat16)
+            own[i] = value[0:128]
+            a_copy(i).start()
+
+        @pl.when((i >= 1) & (i < steps + 1))
+        def _():
+            j = i - 1
+            a_copy(j).wait_recv()
+            value = own[j] + a_recv[j].astype(jnp.float32)
+            for g in (3, 1, 2):
+                b_send[j, g - 1] = value[g * 32 : g * 32 + 32].astype(jnp.bfloat16)
+                b_copy(j, g).start()
+            col[j] = value[0:32]
+
+        @pl.when((i >= 2) & (i < steps + 2))
+        def _():
+            j = i - 2
+            value = col[j]
+            for g in (1, 2, 3):
+                b_copy(j, g).wait_recv()
+                value = value + b_recv[j, g - 1].astype(jnp.float32)
+            for d in (2, 1, 3):
+                line = value[d * 8 : d * 8 + 8]
+                folded = jnp.concatenate([line[:, : CHUNK // 2], line[:, CHUNK // 2 :]], axis=0)
+                c_send[j, d - 1] = folded.astype(jnp.bfloat16)
+                c_copy(j, d).start()
+            col[j, 0:8, :] = value[0:8]
+
+        @pl.when(i >= 3)
+        def _():
+            j = i - 3
+            value = col[j, 0:8, :]
+            for d in (1, 2, 3):
+                c_copy(j, d).wait_recv()
+                folded = c_recv[j, d - 1].astype(jnp.float32)
+                value = value + jnp.concatenate([folded[0:8], folded[8:16]], axis=1)
+            part = pl.ds(pl.multiple_of(j * CHUNK, CHUNK), CHUNK)
+            out[:, part] = value.astype(out.dtype)
+
+    for copy in sent:
+        copy.wait_send()
+
+    @pl.loop(0, steps)
+    def _(j):
+        a_copy(j).wait_send()
+        for g in (1, 2, 3):
+            b_copy(j, g).wait_send()
+        for d in (1, 2, 3):
+            c_copy(j, d).wait_send()
+
+
+def fused_shards(out_grad, routes, gate_weight, gate_proj, up_proj, down_proj, saved_gate, saved_up):
+    feature = out_grad.shape[1]
+    hidden = gate_proj.shape[2]
+    total = saved_gate.shape[1]
+    steps = feature // CHUNK
+    bf16, f32 = jnp.bfloat16, jnp.float32
+    vmem = pl.BlockSpec(memory_space=pltpu.VMEM)
+    anywhere = pl.BlockSpec(memory_space=pl.ANY)
+    dma = pltpu.SemaphoreType.DMA
+    flops = 2 * 3 * total * feature * hidden
+    return pl.pallas_call(
+        fused_kernel,
+        out_shape=jax.ShapeDtypeStruct(out_grad.shape, bf16),
+        in_specs=[vmem] * 3 + [anywhere] * 5,
+        out_specs=vmem,
+        scratch_shapes=[
+            pltpu.VMEM((feature, hidden), bf16),
+            pltpu.VMEM((feature, hidden), bf16),
+            pltpu.VMEM((hidden, feature), bf16),
+            pltpu.VMEM((total, hidden), bf16),
+            pltpu.VMEM((total, hidden), bf16),
+            pltpu.VMEM((32, 16, feature // 2 + META), bf16),
+            pltpu.VMEM((total, feature), bf16),
+            pltpu.VMEM((total, hidden), bf16),
+            pltpu.VMEM((total, hidden), bf16),
+            pltpu.VMEM((steps, 128, CHUNK), f32),
+            pltpu.VMEM((steps, 128, CHUNK), bf16),
+            pltpu.VMEM((steps, 128, CHUNK), bf16),
+            pltpu.VMEM((steps, 32, CHUNK), f32),
+            pltpu.VMEM((steps, 3, 32, CHUNK), bf16),
+            pltpu.VMEM((steps, 3, 32, CHUNK), bf16),
+            pltpu.VMEM((steps, 3, 16, CHUNK // 2), bf16),
+            pltpu.VMEM((steps, 3, 16, CHUNK // 2), bf16),
+            dma((3, max(steps, hidden // CHUNK))),
+            dma((2,)),
+            dma((31,)),
+            dma((32,)),
+            dma((steps,)),
+            dma((steps,)),
+            dma((steps, 3)),
+            dma((steps, 3)),
+            dma((steps, 3)),
+            dma((steps, 3)),
+        ],
+        compiler_params=pltpu.CompilerParams(
+            collective_id=0, has_side_effects=True, vmem_limit_bytes=60 * 1024 * 1024
+        ),
+        cost_estimate=pl.CostEstimate(
+            flops=flops, bytes_accessed=3 * 2 * feature * hidden, transcendentals=total * hidden
+        ),
+    )(out_grad, routes, gate_weight, gate_proj, up_proj, down_proj, saved_gate, saved_up)
 
 
 def rank_slots(flat_routes):
@@ -78,4 +391,6 @@
         P("expert", None, "cuts"),
     )
     out_specs = P(("expert", "cuts"), None)
-    return jax.shard_map(shards, mesh=mesh, in_specs=in_specs, out_specs=out_specs, check_vma=False)
+    fused = (mesh.shape["expert"], mesh.shape["cuts"]) == (4, 8)
+    body = fused_shards if fused else shards
+    return jax.shard_map(body, mesh=mesh, in_specs=in_specs, out_specs=out_specs, check_vma=False)

time: 189 us -> 54.5 us (0.29)
  waiting for transfers between devices: 125 us -> 0 us
  Pallas kernels: 0 us -> 50.1 us
  matrix products: 32.1 us -> 0 us
  between operations: 13.5 us -> 0.01 us
  blocking collectives: 9.45 us -> 0 us
  starting transfers between devices: 3.5 us -> 0 us
    reduce_scatter x1 -> x0, waiting for transfers between devices: 72.6 us -> none  [shards(): lax.psum_scatter(expert_rows(gathered, gate_proj[0], up_proj[0], down_pro...]
    pallas_call x0 -> x1, Pallas kernels: none -> 50.1 us  [fused_shards(): pl.pallas_call(fused_kernel, out_shape=jax.ShapeDtypeStruct(out_grad.shap...]
    all_gather x1 -> x0, waiting for transfers between devices: 45 us -> none  [shards(): lax.all_gather(arrived, 'cuts', axis=0, tiled=True).reshape(-1, feature_dim)]
    dot_general x4 -> x0, matrix products: 32.1 us -> none  [the longest x1 15 us: expert_rows(): lax.dot_general(gate_grad, gate_mat, contract, preferred_element_type=jnp...]
    all_to_all x1 -> x0, blocking collectives: 9.45 us -> none  [shards(): lax.all_to_all(outgoing, 'expert', split_axis=0, concat_axis=0, tiled=True)]
    all_to_all x1 -> x0, waiting for transfers between devices: 7.38 us -> none  [shards(): lax.all_to_all(own_rows, 'expert', split_axis=0, concat_axis=0, tiled=True)]
    all_to_all x1 -> x0, starting transfers between devices: 3.46 us -> none  [shards(): lax.all_to_all(own_rows, 'expert', split_axis=0, concat_axis=0, tiled=True)]
    unnamed x8 -> x3, local copies, waits for them, and re-layouts: 2.18 us -> 4.11 us
  transfers between devices with their start and end apart: 3 -> 0, of which waited for: 3 -> 0; matrix products, arithmetic and copies ran while one was open for 0% -> 0% of each run, Pallas kernels for 0% -> 0%
where the time goes in v1:
time: 54.5 us; the launch traced here: 54.2 us
  Pallas kernels  50.1 us (92%)
  local copies, waits for them, and re-layouts  4.11 us (8%)
    pallas_call x1, Pallas kernels, fused_shards(): pl.pallas_call(fused_kernel, out_shape=jax.ShapeDtypeStruct(out_grad.shap...  50.1 us
    unnamed x3, local copies, waits for them, and re-layouts  4.11 us

profile of v1, /device:TPU:0, one launch (start us, length us, event | category | flops | bytes accessed | tf_op | source)
XLA Modules:
  0.0 54.2 jit_solution(6670740967072100777)
XLA Ops:
  0.0 1.3 %copy.9.routes = s32[8,2]{1,0:T(8,128)} copy(s32[8,2]{0,1:T(2,128)} %param.9) | data formatting | bytes 128 | tf_op args[1]
  1.3 1.3 %copy.10.gates = f32[8,2]{1,0:T(8,128)} copy(f32[8,2]{0,1:T(2,128)} %param.10) | data formatting | bytes 128 | tf_op args[2]
  2.7 50.1 %shard_map.82 = bf16[8,3072]{1,0:T(8,128)(2,1)} custom-call(bf16[8,3072]{1,0:T(8,128)(2,1)} %tok.1, s32[8,2]{1,0:T(8,128)} %copy.9.routes, f32[8,2]{1,0:T(8,128)} %copy.10.gates, bf16[1,3072,2048]{2,1,0:T(8,128)(2,1)} %gate_hbm.1, bf16[1,3072,2048]{2,1,0:T(8,128)(2,1)} %up_hbm.1, bf16[1,2048,3072]{2,1,0:T(8,128)(2,1)} %down_hbm.1, ...), custom_call_target="tpu_custom_call" | custom-call | flops 9663676416 | bytes 37748736 | tf_op jit(solution)/shard_map/pallas_call | solution.py:277
  52.8 1.4 %copy.12 = bf16[8,3072]{1,0:T(8,128)(2,1)} copy(bf16[8,3072]{1,0:T(8,128)(2,1)} %shard_map.82) | data formatting | bytes 98304

commit v2 on v1

--- a/solution.py
+++ b/solution.py
@@ -6,9 +6,15 @@
 from jax.sharding import PartitionSpec as P
 
 MESH = pl.DeviceIdType.MESH
-TRANSPOSED = (((1,), (1,)), ((), ()))
+LEADING = (((0,), (0,)), ((), ()))
 META = 128
 CHUNK = 512
+
+
+def upright(ref, choice):
+    across = jnp.broadcast_to(ref[choice : choice + 1, :].astype(jnp.float32), (8, 8))
+    keep = lax.broadcasted_iota(jnp.int32, (8, 8), 0) == lax.broadcasted_iota(jnp.int32, (8, 8), 1)
+    return jnp.sum(jnp.where(keep, across, 0.0), axis=1, keepdims=True)
 
 
 def fused_kernel(
@@ -24,7 +30,7 @@
     feature = tok.shape[1]
     half = feature // 2
     hidden = down_v.shape[0]
-    total = rows.shape[0]
+    total = rows.shape[1]
     steps = feature // CHUNK
     hidden_steps = hidden // CHUNK
 
@@ -34,7 +40,10 @@
         ((1 - x) * 2 + core, cut),
         ((1 - x) * 2 + core, z * 2 + (1 - y)),
     ]
-    depth = [None] + [(expert, ((z + d) % 4) * 2 + y) for d in (1, 2, 3)]
+    z_high, z_low = z // 2, z % 2
+    depth = [None] + [
+        (expert, (((z_high + d // 2) % 2) * 2 + (z_low + d % 2) % 2) * 2 + y) for d in (1, 2, 3)
+    ]
     twin = (x * 2 + (1 - core), cut)
 
     def down_copy(n):
@@ -69,10 +78,10 @@
     lane = lax.broadcasted_iota(jnp.int32, (8, META), 1)
     level = lane // 32
     name = lane % 32
-    first = (routes[:, 0:1] == name).astype(jnp.float32)
-    second = (routes[:, 1:2] == name).astype(jnp.float32)
+    first = (upright(routes, 0) == name.astype(jnp.float32)).astype(jnp.float32)
+    second = (upright(routes, 1) == name.astype(jnp.float32)).astype(jnp.float32)
     hit = first + second
-    weight = first * gates[:, 0:1] + second * gates[:, 1:2]
+    weight = first * upright(gates, 0) + second * upright(gates, 1)
     sub = lax.broadcasted_iota(jnp.int32, (8, META), 0)
     slot = jnp.zeros((8, META), jnp.float32)
     for t in range(7):
@@ -116,19 +125,30 @@
         ).wait_recv()
 
     sent = []
-    for d in (1, 3, 2):
-        sent.append(send(0, 4 - d, depth[d], len(sent)))
-    for d in (0, 1, 3, 2):
+    order = (0, 2, 1, 3)
+    for d in (2, 1, 3):
+        sent.append(send(0, d, depth[d], len(sent)))
+    for d in order:
         if d:
             arrived(d)
-        for g in (3, 1, 2):
+        for g in (3, 1, 2) if d in (0, 2) else (1, 2):
             sent.append(send(d, g * 4 + d, column[g], len(sent)))
         sent.append(send(d, 16 + d, twin, len(sent)))
-    for d in (0, 1, 3, 2):
-        for g in (1, 2, 3):
+        if d == 1:
+            arrived(12)
+            sent.append(send(12, 13, depth[1], len(sent)))
+            sent.append(send(12, 28, twin, len(sent)))
+    arrived(14)
+    sent.append(send(14, 15, depth[1], len(sent)))
+    sent.append(send(14, 30, twin, len(sent)))
+    for d in order:
+        for g in (1, 2):
             arrived(g * 4 + d)
             sent.append(send(g * 4 + d, 16 + g * 4 + d, twin, len(sent)))
-    for d in (0, 1, 3, 2):
+    for d in (1, 3):
+        arrived(12 + d)
+        sent.append(send(12 + d, 28 + d, twin, len(sent)))
+    for d in order:
         for g in range(4):
             arrived(16 + g * 4 + d)
 
@@ -142,10 +162,10 @@
     far_core = (core + place // 128) % 2
     far_x = (x + (place // 64) % 2) % 2
     far_y = (y + (place // 32) % 2) % 2
-    far_z = (z + (place // 8) % 4) % 4
+    far_z = ((z_high + (place // 16) % 2) % 2) * 2 + (z_low + (place // 8) % 2) % 2
     base = ((far_z * 2 + far_y) * 4 + far_x * 2 + far_core) * 8
     spot = lax.broadcasted_iota(jnp.int32, (total, total), 1) - base
-    placing = (spot.astype(jnp.float32) == slot).astype(jnp.bfloat16)
+    placing = (spot.astype(jnp.float32) == slot).astype(jnp.float32).T.astype(jnp.bfloat16)
 
     quarter = half // 4
     for n in range(4):
@@ -153,7 +173,7 @@
         for h in range(2):
             value = part[:, h * 8 : h * 8 + 8, :].reshape(total, quarter) * weight
             start = h * half + n * quarter
-            rows[:, start : start + quarter] = value.astype(jnp.bfloat16)
+            rows[start : start + quarter, :] = value.astype(jnp.bfloat16).T
 
     for copy in saved:
         copy.wait()
@@ -162,14 +182,14 @@
     def _(n):
         down_copy(n).wait()
         part = pl.ds(pl.multiple_of(n * CHUNK, CHUNK), CHUNK)
-        grad = lax.dot_general(
-            rows[...], down_v[part, :], TRANSPOSED, preferred_element_type=jnp.float32
+        grad = jnp.dot(down_v[part, :], rows[...], preferred_element_type=jnp.float32)
+        a = lax.dot_general(
+            sgate_v[:, part], placing, LEADING, preferred_element_type=jnp.float32
         )
-        a = jnp.dot(placing, sgate_v[:, part], preferred_element_type=jnp.float32)
-        b = jnp.dot(placing, sup_v[:, part], preferred_element_type=jnp.float32)
+        b = lax.dot_general(sup_v[:, part], placing, LEADING, preferred_element_type=jnp.float32)
         q = jax.nn.sigmoid(a)
-        up_g[:, part] = (grad * a * q).astype(jnp.bfloat16)
-        gate_g[:, part] = (grad * b * q * (1.0 + a * (1.0 - q))).astype(jnp.bfloat16)
+        up_g[part, :] = (grad * a * q).astype(jnp.bfloat16)
+        gate_g[part, :] = (grad * b * q * (1.0 + a * (1.0 - q))).astype(jnp.bfloat16)
 
     def a_copy(j):
         return pltpu.make_async_remote_copy(
@@ -208,11 +228,10 @@
             gate_copy(i).wait()
             up_copy(i).wait()
             part = pl.ds(pl.multiple_of(i * CHUNK, CHUNK), CHUNK)
-            value = lax.dot_general(
-                gate_g[...], gate_v[part, :], TRANSPOSED, preferred_element_type=jnp.float32
-            ) + lax.dot_general(
-                up_g[...], up_v[part, :], TRANSPOSED, preferred_element_type=jnp.float32
-            )
+            value = jnp.dot(
+                gate_v[part, :], gate_g[...], preferred_element_type=jnp.float32
+            ) + jnp.dot(up_v[part, :], up_g[...], preferred_element_type=jnp.float32)
+            value = value.T
             a_send[i] = value[128:256].astype(jnp.bfloat16)
             own[i] = value[0:128]
             a_copy(i).start()
@@ -286,9 +305,9 @@
             pltpu.VMEM((total, hidden), bf16),
             pltpu.VMEM((total, hidden), bf16),
             pltpu.VMEM((32, 16, feature // 2 + META), bf16),
-            pltpu.VMEM((total, feature), bf16),
-            pltpu.VMEM((total, hidden), bf16),
-            pltpu.VMEM((total, hidden), bf16),
+            pltpu.VMEM((feature, total), bf16),
+            pltpu.VMEM((hidden, total), bf16),
+            pltpu.VMEM((hidden, total), bf16),
             pltpu.VMEM((steps, 128, CHUNK), f32),
             pltpu.VMEM((steps, 128, CHUNK), bf16),
             pltpu.VMEM((steps, 128, CHUNK), bf16),
@@ -314,7 +333,7 @@
         cost_estimate=pl.CostEstimate(
             flops=flops, bytes_accessed=3 * 2 * feature * hidden, transcendentals=total * hidden
         ),
-    )(out_grad, routes, gate_weight, gate_proj, up_proj, down_proj, saved_gate, saved_up)
+    )(out_grad, routes.T, gate_weight.T, gate_proj, up_proj, down_proj, saved_gate, saved_up)
 
 
 def rank_slots(flat_routes):

time: 54.5 us -> 50.6 us (0.928)
  local copies, waits for them, and re-layouts: 4.11 us -> 1.42 us
  Pallas kernels: 50.1 us -> 49 us
    unnamed x3 -> x1, local copies, waits for them, and re-layouts: 4.11 us -> 1.42 us
    pallas_call x1, Pallas kernels: 50.1 us -> 49 us  [fused_shards(): pl.pallas_call(fused_kernel, out_shape=jax.ShapeDtypeStruct(out_grad.shap...]
where the time goes in v2:
time: 50.6 us; the launch traced here: 50.4 us
  Pallas kernels  49 us (97%)
  local copies, waits for them, and re-layouts  1.42 us (3%)
    pallas_call x1, Pallas kernels, fused_shards(): pl.pallas_call(fused_kernel, out_shape=jax.ShapeDtypeStruct(out_grad.shap...  49 us
    unnamed x1, local copies, waits for them, and re-layouts  1.42 us

profile of v2, /device:TPU:0, one launch (start us, length us, event | category | flops | bytes accessed | tf_op | source)
XLA Modules:
  0.0 50.4 jit_solution(2491603444999767824)
XLA Ops:
  0.0 49.0 %shard_map.82 = bf16[8,3072]{1,0:T(8,128)(2,1)} custom-call(bf16[8,3072]{1,0:T(8,128)(2,1)} %tok.1, s32[2,8]{1,0:T(2,128)} %bitcast.2, f32[2,8]{1,0:T(2,128)} %bitcast.3, bf16[1,3072,2048]{2,1,0:T(8,128)(2,1)} %gate_hbm.1, bf16[1,3072,2048]{2,1,0:T(8,128)(2,1)} %up_hbm.1, bf16[1,2048,3072]{2,1,0:T(8,128)(2,1)} %down_hbm.1, bf16[1,256,2048]{2,1,0:T(8,128)(2,1)} %sgate_hbm.1, ...), custom_call_target="tpu_custom_call" | custom-call | flops 9663676416 | bytes 37748736 | tf_op jit(solution)/shard_map/pallas_call | solution.py:296
  49.0 1.4 %copy.10 = bf16[8,3072]{1,0:T(8,128)(2,1)} copy(bf16[8,3072]{1,0:T(8,128)(2,1)} %shard_map.82) | data formatting | bytes 98304

commit v3 on v2

--- a/solution.py
+++ b/solution.py
@@ -19,9 +19,9 @@
 
 def fused_kernel(
     tok, routes, gates, gate_hbm, up_hbm, down_hbm, sgate_hbm, sup_hbm, out,
-    gate_v, up_v, down_v, sgate_v, sup_v, blocks, rows, gate_g, up_g,
+    gate_v, up_v, down_v, sgate_v, sup_v, blocks, meta, rows, gate_g, up_g, gate_f, up_f,
     own, a_send, a_recv, col, b_send, b_recv, c_send, c_recv,
-    w_sem, s_sem, gs_sem, gr_sem, as_sem, ar_sem, bs_sem, br_sem, cs_sem, cr_sem,
+    w_sem, s_sem, ms_sem, mr_sem, gs_sem, gr_sem, as_sem, ar_sem, bs_sem, br_sem, cs_sem, cr_sem,
 ):
     expert = lax.axis_index("expert")
     cut = lax.axis_index("cuts")
@@ -71,9 +71,6 @@
         copy.start()
     for n in range(hidden_steps):
         down_copy(n).start()
-    for n in range(steps):
-        gate_copy(n).start()
-        up_copy(n).start()
 
     lane = lax.broadcasted_iota(jnp.int32, (8, META), 1)
     level = lane // 32
@@ -90,15 +87,13 @@
     high = weight.astype(jnp.bfloat16).astype(jnp.float32)
     middle = (weight - high).astype(jnp.bfloat16).astype(jnp.float32)
     low = weight - high - middle
-    meta = jnp.where(
+    routing = jnp.where(
         level == 0, high, jnp.where(level == 1, middle, jnp.where(level == 2, low, slot))
     )
+    meta[0] = jnp.concatenate([routing, jnp.zeros_like(routing)], axis=0).astype(jnp.bfloat16)
     tokens = tok[...].astype(jnp.float32)
     stacked = jnp.concatenate([tokens[:, :half], tokens[:, half:]], axis=0)
-    blocks[0, :, 0:half] = stacked.astype(jnp.bfloat16)
-    blocks[0, :, half : half + META] = jnp.concatenate(
-        [meta, jnp.zeros_like(meta)], axis=0
-    ).astype(jnp.bfloat16)
+    blocks[0] = stacked.astype(jnp.bfloat16)
 
     pl.semaphore_wait(barrier, 7)
 
@@ -125,35 +120,50 @@
         ).wait_recv()
 
     sent = []
+    def meta_copy(n, source, target, count, peer):
+        return pltpu.make_async_remote_copy(
+            src_ref=meta.at[pl.ds(source, count)],
+            dst_ref=meta.at[pl.ds(target, count)],
+            send_sem=ms_sem.at[n],
+            recv_sem=mr_sem.at[n],
+            device_id=peer,
+            device_id_type=MESH,
+        )
+
+    meta_depth = [meta_copy(d - 1, 0, d, 1, depth[d]) for d in (1, 2, 3)]
+    meta_column = [meta_copy(2 + g, 0, g * 4, 4, column[g]) for g in (1, 2, 3)]
+    meta_twin = meta_copy(6, 0, 16, 16, twin)
+
+    def to_twin(index):
+        sent.append(send(index, 16 + index, twin, len(sent)))
+
+    for copy in meta_depth:
+        copy.start()
     order = (0, 2, 1, 3)
     for d in (2, 1, 3):
         sent.append(send(0, d, depth[d], len(sent)))
+    for copy in meta_depth:
+        copy.wait_recv()
+    for copy in meta_column:
+        copy.start()
     for d in order:
         if d:
             arrived(d)
         for g in (3, 1, 2) if d in (0, 2) else (1, 2):
             sent.append(send(d, g * 4 + d, column[g], len(sent)))
-        sent.append(send(d, 16 + d, twin, len(sent)))
-        if d == 1:
-            arrived(12)
-            sent.append(send(12, 13, depth[1], len(sent)))
-            sent.append(send(12, 28, twin, len(sent)))
-    arrived(14)
-    sent.append(send(14, 15, depth[1], len(sent)))
-    sent.append(send(14, 30, twin, len(sent)))
-    for d in order:
-        for g in (1, 2):
-            arrived(g * 4 + d)
-            sent.append(send(g * 4 + d, 16 + g * 4 + d, twin, len(sent)))
-    for d in (1, 3):
-        arrived(12 + d)
-        sent.append(send(12 + d, 28 + d, twin, len(sent)))
-    for d in order:
-        for g in range(4):
-            arrived(16 + g * 4 + d)
-
-    info = blocks[:, :, half : half + META].astype(jnp.float32)[:, 0:8, :]
-    info = info.reshape(total, META)
+        to_twin(d)
+    for n in range(steps):
+        gate_copy(n).start()
+        up_copy(n).start()
+    for copy in meta_column:
+        copy.wait_recv()
+    meta_twin.start()
+    arrived(12)
+    sent.append(send(12, 13, depth[1], len(sent)))
+    to_twin(12)
+    meta_twin.wait_recv()
+
+    info = meta[...].astype(jnp.float32)[:, 0:8, :].reshape(total, META)
     lane = lax.broadcasted_iota(jnp.int32, (total, META), 1)
     mine = (lane % 32) == expert
     weight = jnp.sum(jnp.where(mine & (lane < 96), info, 0.0), axis=1, keepdims=True)
@@ -167,29 +177,50 @@
     spot = lax.broadcasted_iota(jnp.int32, (total, total), 1) - base
     placing = (spot.astype(jnp.float32) == slot).astype(jnp.float32).T.astype(jnp.bfloat16)
 
-    quarter = half // 4
-    for n in range(4):
-        part = blocks[:, :, n * quarter : (n + 1) * quarter].astype(jnp.float32)
-        for h in range(2):
-            value = part[:, h * 8 : h * 8 + 8, :].reshape(total, quarter) * weight
-            start = h * half + n * quarter
-            rows[start : start + quarter, :] = value.astype(jnp.bfloat16).T
-
     for copy in saved:
         copy.wait()
+    for n in range(4):
+        size = hidden // 4
+        part = slice(n * size, (n + 1) * size)
+        a = lax.dot_general(
+            sgate_v[:, part], placing, LEADING, preferred_element_type=jnp.float32
+        )
+        b = lax.dot_general(sup_v[:, part], placing, LEADING, preferred_element_type=jnp.float32)
+        q = jax.nn.sigmoid(a)
+        up_f[part, :] = a * q
+        gate_f[part, :] = b * q * (1.0 + a * (1.0 - q))
+        for g in (1, 2):
+            arrived(g * 4 + order[n])
+            to_twin(g * 4 + order[n])
+        if n == 0:
+            arrived(14)
+            sent.append(send(14, 15, depth[1], len(sent)))
+            to_twin(14)
+    for d in (1, 3):
+        arrived(12 + d)
+        to_twin(12 + d)
+
+    quarter = half // 4
+    for k in range(2):
+        if k == 1:
+            for index in range(16, 32):
+                arrived(index)
+        span = slice(k * 128, (k + 1) * 128)
+        for n in range(4):
+            part = blocks[k * 16 : k * 16 + 16, :, n * quarter : (n + 1) * quarter]
+            part = part.astype(jnp.float32)
+            for h in range(2):
+                value = part[:, h * 8 : h * 8 + 8, :].reshape(128, quarter) * weight[span]
+                start = h * half + n * quarter
+                rows[start : start + quarter, span] = value.astype(jnp.bfloat16).T
 
     @pl.loop(0, hidden_steps)
     def _(n):
         down_copy(n).wait()
         part = pl.ds(pl.multiple_of(n * CHUNK, CHUNK), CHUNK)
         grad = jnp.dot(down_v[part, :], rows[...], preferred_element_type=jnp.float32)
-        a = lax.dot_general(
-            sgate_v[:, part], placing, LEADING, preferred_element_type=jnp.float32
-        )
-        b = lax.dot_general(sup_v[:, part], placing, LEADING, preferred_element_type=jnp.float32)
-        q = jax.nn.sigmoid(a)
-        up_g[part, :] = (grad * a * q).astype(jnp.bfloat16)
-        gate_g[part, :] = (grad * b * q * (1.0 + a * (1.0 - q))).astype(jnp.bfloat16)
+        up_g[part, :] = (grad * up_f[part, :]).astype(jnp.bfloat16)
+        gate_g[part, :] = (grad * gate_f[part, :]).astype(jnp.bfloat16)
 
     def a_copy(j):
         return pltpu.make_async_remote_copy(
@@ -271,7 +302,7 @@
             part = pl.ds(pl.multiple_of(j * CHUNK, CHUNK), CHUNK)
             out[:, part] = value.astype(out.dtype)
 
-    for copy in sent:
+    for copy in sent + meta_depth + meta_column + [meta_twin]:
         copy.wait_send()
 
     @pl.loop(0, steps)
@@ -304,10 +335,13 @@
             pltpu.VMEM((hidden, feature), bf16),
             pltpu.VMEM((total, hidden), bf16),
             pltpu.VMEM((total, hidden), bf16),
-            pltpu.VMEM((32, 16, feature // 2 + META), bf16),
+            pltpu.VMEM((32, 16, feature // 2), bf16),
+            pltpu.VMEM((32, 16, META), bf16),
             pltpu.VMEM((feature, total), bf16),
             pltpu.VMEM((hidden, total), bf16),
             pltpu.VMEM((hidden, total), bf16),
+            pltpu.VMEM((hidden, total), f32),
+            pltpu.VMEM((hidden, total), f32),
             pltpu.VMEM((steps, 128, CHUNK), f32),
             pltpu.VMEM((steps, 128, CHUNK), bf16),
             pltpu.VMEM((steps, 128, CHUNK), bf16),
@@ -318,6 +352,8 @@
             pltpu.VMEM((steps, 3, 16, CHUNK // 2), bf16),
             dma((3, max(steps, hidden // CHUNK))),
             dma((2,)),
+            dma((7,)),
+            dma((7,)),
             dma((31,)),
             dma((32,)),
             dma((steps,)),

time: 50.6 us -> 51 us (level)
  no operation moved by 1% of the time
where the time goes in v3:
time: 51 us; the launch traced here: 50.8 us
  Pallas kernels  49.3 us (97%)
  local copies, waits for them, and re-layouts  1.42 us (3%)
    pallas_call x1, Pallas kernels, fused_shards(): pl.pallas_call(fused_kernel, out_shape=jax.ShapeDtypeStruct(out_grad.shap...  49.3 us
    unnamed x1, local copies, waits for them, and re-layouts  1.42 us

profile of v3, /device:TPU:0, one launch (start us, length us, event | category | flops | bytes accessed | tf_op | source)
XLA Modules:
  0.0 50.8 jit_solution(4313341450543979167)
XLA Ops:
  0.0 49.3 %shard_map.82 = bf16[8,3072]{1,0:T(8,128)(2,1)} custom-call(bf16[8,3072]{1,0:T(8,128)(2,1)} %tok.1, s32[2,8]{1,0:T(2,128)} %bitcast.2, f32[2,8]{1,0:T(2,128)} %bitcast.3, bf16[1,3072,2048]{2,1,0:T(8,128)(2,1)} %gate_hbm.1, bf16[1,3072,2048]{2,1,0:T(8,128)(2,1)} %up_hbm.1, bf16[1,2048,3072]{2,1,0:T(8,128)(2,1)} %down_hbm.1, bf16[1,256,2048]{2,1,0:T(8,128)(2,1)} %sgate_hbm.1, ...), custom_call_target="tpu_custom_call" | custom-call | flops 9663676416 | bytes 37748736 | tf_op jit(solution)/shard_map/pallas_call | solution.py:327
  49.3 1.4 %copy.10 = bf16[8,3072]{1,0:T(8,128)(2,1)} copy(bf16[8,3072]{1,0:T(8,128)(2,1)} %shard_map.82) | data formatting | bytes 98304

commit v4 on v3

--- a/solution.py
+++ b/solution.py
@@ -71,6 +71,9 @@
         copy.start()
     for n in range(hidden_steps):
         down_copy(n).start()
+    for n in range(steps):
+        gate_copy(n).start()
+        up_copy(n).start()
 
     lane = lax.broadcasted_iota(jnp.int32, (8, META), 1)
     level = lane // 32
@@ -152,9 +155,6 @@
         for g in (3, 1, 2) if d in (0, 2) else (1, 2):
             sent.append(send(d, g * 4 + d, column[g], len(sent)))
         to_twin(d)
-    for n in range(steps):
-        gate_copy(n).start()
-        up_copy(n).start()
     for copy in meta_column:
         copy.wait_recv()
     meta_twin.start()
@@ -252,7 +252,7 @@
             device_id_type=MESH,
         )
 
-    @pl.loop(0, steps + 3)
+    @pl.loop(0, steps + 5)
     def _(i):
         @pl.when(i < steps)
         def _():
@@ -277,9 +277,9 @@
                 b_copy(j, g).start()
             col[j] = value[0:32]
 
-        @pl.when((i >= 2) & (i < steps + 2))
+        @pl.when((i >= 3) & (i < steps + 3))
         def _():
-            j = i - 2
+            j = i - 3
             value = col[j]
             for g in (1, 2, 3):
                 b_copy(j, g).wait_recv()
@@ -291,9 +291,9 @@
                 c_copy(j, d).start()
             col[j, 0:8, :] = value[0:8]
 
-        @pl.when(i >= 3)
+        @pl.when(i >= 5)
         def _():
-            j = i - 3
+            j = i - 5
             value = col[j, 0:8, :]
             for d in (1, 2, 3):
                 c_copy(j, d).wait_recv()

time: 51 us -> 47.1 us (0.924)
  Pallas kernels: 49.3 us -> 45.4 us
    pallas_call x1, Pallas kernels: 49.3 us -> 45.4 us  [fused_shards(): pl.pallas_call(fused_kernel, out_shape=jax.ShapeDtypeStruct(out_grad.shap...]
where the time goes in v4:
time: 47.1 us; the launch traced here: 46.9 us
  Pallas kernels  45.4 us (96%)
  local copies, waits for them, and re-layouts  1.42 us (3%)
    pallas_call x1, Pallas kernels, fused_shards(): pl.pallas_call(fused_kernel, out_shape=jax.ShapeDtypeStruct(out_grad.shap...  45.4 us
    unnamed x1, local copies, waits for them, and re-layouts  1.42 us

profile of v4, /device:TPU:0, one launch (start us, length us, event | category | flops | bytes accessed | tf_op | source)
XLA Modules:
  0.0 46.9 jit_solution(4163212126051313029)
XLA Ops:
  0.0 45.4 %shard_map.82 = bf16[8,3072]{1,0:T(8,128)(2,1)} custom-call(bf16[8,3072]{1,0:T(8,128)(2,1)} %tok.1, s32[2,8]{1,0:T(2,128)} %bitcast.2, f32[2,8]{1,0:T(2,128)} %bitcast.3, bf16[1,3072,2048]{2,1,0:T(8,128)(2,1)} %gate_hbm.1, bf16[1,3072,2048]{2,1,0:T(8,128)(2,1)} %up_hbm.1, bf16[1,2048,3072]{2,1,0:T(8,128)(2,1)} %down_hbm.1, bf16[1,256,2048]{2,1,0:T(8,128)(2,1)} %sgate_hbm.1, ...), custom_call_target="tpu_custom_call" | custom-call | flops 9663676416 | bytes 37748736 | tf_op jit(solution)/shard_map/pallas_call | solution.py:327
  45.4 1.4 %copy.10 = bf16[8,3072]{1,0:T(8,128)(2,1)} copy(bf16[8,3072]{1,0:T(8,128)(2,1)} %shard_map.82) | data formatting | bytes 98304

commit v5 on v4

--- a/solution.py
+++ b/solution.py
@@ -262,16 +262,15 @@
             value = jnp.dot(
                 gate_v[part, :], gate_g[...], preferred_element_type=jnp.float32
             ) + jnp.dot(up_v[part, :], up_g[...], preferred_element_type=jnp.float32)
-            value = value.T
-            a_send[i] = value[128:256].astype(jnp.bfloat16)
-            own[i] = value[0:128]
+            a_send[i] = value[:, 128:256].astype(jnp.bfloat16)
             a_copy(i).start()
+            own[i] = value[:, 0:128]
 
         @pl.when((i >= 1) & (i < steps + 1))
         def _():
             j = i - 1
             a_copy(j).wait_recv()
-            value = own[j] + a_recv[j].astype(jnp.float32)
+            value = (own[j] + a_recv[j].astype(jnp.float32)).T
             for g in (3, 1, 2):
                 b_send[j, g - 1] = value[g * 32 : g * 32 + 32].astype(jnp.bfloat16)
                 b_copy(j, g).start()
@@ -342,9 +341,9 @@
             pltpu.VMEM((hidden, total), bf16),
             pltpu.VMEM((hidden, total), f32),
             pltpu.VMEM((hidden, total), f32),
-            pltpu.VMEM((steps, 128, CHUNK), f32),
-            pltpu.VMEM((steps, 128, CHUNK), bf16),
-            pltpu.VMEM((steps, 128, CHUNK), bf16),
+            pltpu.VMEM((steps, CHUNK, 128), f32),
+            pltpu.VMEM((steps, CHUNK, 128), bf16),
+            pltpu.VMEM((steps, CHUNK, 128), bf16),
             pltpu.VMEM((steps, 32, CHUNK), f32),
             pltpu.VMEM((steps, 3, 32, CHUNK), bf16),
             pltpu.VMEM((steps, 3, 32, CHUNK), bf16),

time: 47.1 us -> 47.2 us (level)
  no operation moved by 1% of the time
where the time goes in v5:
time: 47.2 us; the launch traced here: 47 us
  Pallas kernels  45.6 us (97%)
  local copies, waits for them, and re-layouts  1.42 us (3%)
    pallas_call x1, Pallas kernels, fused_shards(): pl.pallas_call(fused_kernel, out_shape=jax.ShapeDtypeStruct(out_grad.shap...  45.6 us
    unnamed x1, local copies, waits for them, and re-layouts  1.42 us

profile of v5, /device:TPU:0, one launch (start us, length us, event | category | flops | bytes accessed | tf_op | source)
XLA Modules:
  0.0 47.0 jit_solution(3011876820096748455)
XLA Ops:
  0.0 45.6 %shard_map.82 = bf16[8,3072]{1,0:T(8,128)(2,1)} custom-call(bf16[8,3072]{1,0:T(8,128)(2,1)} %tok.1, s32[2,8]{1,0:T(2,128)} %bitcast.2, f32[2,8]{1,0:T(2,128)} %bitcast.3, bf16[1,3072,2048]{2,1,0:T(8,128)(2,1)} %gate_hbm.1, bf16[1,3072,2048]{2,1,0:T(8,128)(2,1)} %up_hbm.1, bf16[1,2048,3072]{2,1,0:T(8,128)(2,1)} %down_hbm.1, bf16[1,256,2048]{2,1,0:T(8,128)(2,1)} %sgate_hbm.1, ...), custom_call_target="tpu_custom_call" | custom-call | flops 9663676416 | bytes 37748736 | tf_op jit(solution)/shard_map/pallas_call | solution.py:326
  45.6 1.4 %copy.10 = bf16[8,3072]{1,0:T(8,128)(2,1)} copy(bf16[8,3072]{1,0:T(8,128)(2,1)} %shard_map.82) | data formatting | bytes 98304

commit v6 on v5

--- a/solution.py
+++ b/solution.py
@@ -232,13 +232,16 @@
             device_id_type=MESH,
         )
 
-    def b_copy(j, g):
+    def b_copy(j, leg):
+        along_y = (j + leg) % 2
+        peer = (((x + 1 - along_y) % 2) * 2 + core, z * 2 + (y + along_y) % 2)
+        part = pl.ds(0, 64) if leg == 0 else pl.ds(64, 32)
         return pltpu.make_async_remote_copy(
-            src_ref=b_send.at[j, g - 1],
-            dst_ref=b_recv.at[j, g - 1],
-            send_sem=bs_sem.at[j, g - 1],
-            recv_sem=br_sem.at[j, g - 1],
-            device_id=column[g],
+            src_ref=b_send.at[j, part],
+            dst_ref=b_recv.at[j, part],
+            send_sem=bs_sem.at[j, leg],
+            recv_sem=br_sem.at[j, leg],
+            device_id=peer,
             device_id_type=MESH,
         )
 
@@ -271,18 +274,28 @@
             j = i - 1
             a_copy(j).wait_recv()
             value = (own[j] + a_recv[j].astype(jnp.float32)).T
-            for g in (3, 1, 2):
-                b_send[j, g - 1] = value[g * 32 : g * 32 + 32].astype(jnp.bfloat16)
-                b_copy(j, g).start()
-            col[j] = value[0:32]
+            odd = (j % 2) == 1
+            along_y, along_x = value[32:64], value[64:96]
+            b_send[j, 0:32, :] = jnp.where(odd, along_y, along_x).astype(jnp.bfloat16)
+            b_send[j, 32:64, :] = value[96:128].astype(jnp.bfloat16)
+            b_copy(j, 0).start()
+            col[j, 0:32, :] = value[0:32]
+            col[j, 32:64, :] = jnp.where(odd, along_x, along_y)
 
         @pl.when((i >= 3) & (i < steps + 3))
         def _():
             j = i - 3
-            value = col[j]
-            for g in (1, 2, 3):
-                b_copy(j, g).wait_recv()
-                value = value + b_recv[j, g - 1].astype(jnp.float32)
+            b_copy(j, 0).wait_recv()
+            value = col[j] + b_recv[j, 0:64, :].astype(jnp.float32)
+            b_send[j, 64:96, :] = value[32:64].astype(jnp.bfloat16)
+            b_copy(j, 1).start()
+            col[j, 0:32, :] = value[0:32]
+
+        @pl.when((i >= 4) & (i < steps + 4))
+        def _():
+            j = i - 4
+            b_copy(j, 1).wait_recv()
+            value = col[j, 0:32, :] + b_recv[j, 64:96, :].astype(jnp.float32)
             for d in (2, 1, 3):
                 line = value[d * 8 : d * 8 + 8]
                 folded = jnp.concatenate([line[:, : CHUNK // 2], line[:, CHUNK // 2 :]], axis=0)
@@ -307,8 +320,8 @@
     @pl.loop(0, steps)
     def _(j):
         a_copy(j).wait_send()
-        for g in (1, 2, 3):
-            b_copy(j, g).wait_send()
+        for leg in (0, 1):
+            b_copy(j, leg).wait_send()
         for d in (1, 2, 3):
             c_copy(j, d).wait_send()
 
@@ -344,9 +357,9 @@
             pltpu.VMEM((steps, CHUNK, 128), f32),
             pltpu.VMEM((steps, CHUNK, 128), bf16),
             pltpu.VMEM((steps, CHUNK, 128), bf16),
-            pltpu.VMEM((steps, 32, CHUNK), f32),
-            pltpu.VMEM((steps, 3, 32, CHUNK), bf16),
-            pltpu.VMEM((steps, 3, 32, CHUNK), bf16),
+            pltpu.VMEM((steps, 64, CHUNK), f32),
+            pltpu.VMEM((steps, 96, CHUNK), bf16),
+            pltpu.VMEM((steps, 96, CHUNK), bf16),
             pltpu.VMEM((steps, 3, 16, CHUNK // 2), bf16),
             pltpu.VMEM((steps, 3, 16, CHUNK // 2), bf16),
             dma((3, max(steps, hidden // CHUNK))),
@@ -357,8 +370,8 @@
             dma((32,)),
             dma((steps,)),
             dma((steps,)),
-            dma((steps, 3)),
-            dma((steps, 3)),
+            dma((steps, 2)),
+            dma((steps, 2)),
             dma((steps, 3)),
             dma((steps, 3)),
         ],

time: 47.2 us -> 52.4 us (1.11)
  Pallas kernels: 45.6 us -> 50.8 us
    pallas_call x1, Pallas kernels: 45.6 us -> 50.8 us  [fused_shards(): pl.pallas_call(fused_kernel, out_shape=jax.ShapeDtypeStruct(out_grad.shap...]
where the time goes in v6:
time: 52.4 us; the launch traced here: 52.2 us
  Pallas kernels  50.8 us (97%)
  local copies, waits for them, and re-layouts  1.42 us (3%)
    pallas_call x1, Pallas kernels, fused_shards(): pl.pallas_call(fused_kernel, out_shape=jax.ShapeDtypeStruct(out_grad.shap...  50.8 us
    unnamed x1, local copies, waits for them, and re-layouts  1.42 us

profile of v6, /device:TPU:0, one launch (start us, length us, event | category | flops | bytes accessed | tf_op | source)
XLA Modules:
  0.0 52.2 jit_solution(16539916280637228684)
XLA Ops:
  0.0 50.8 %shard_map.82 = bf16[8,3072]{1,0:T(8,128)(2,1)} custom-call(bf16[8,3072]{1,0:T(8,128)(2,1)} %tok.1, s32[2,8]{1,0:T(2,128)} %bitcast.2, f32[2,8]{1,0:T(2,128)} %bitcast.3, bf16[1,3072,2048]{2,1,0:T(8,128)(2,1)} %gate_hbm.1, bf16[1,3072,2048]{2,1,0:T(8,128)(2,1)} %up_hbm.1, bf16[1,2048,3072]{2,1,0:T(8,128)(2,1)} %down_hbm.1, bf16[1,256,2048]{2,1,0:T(8,128)(2,1)} %sgate_hbm.1, ...), custom_call_target="tpu_custom_call" | custom-call | flops 9663676416 | bytes 37748736 | tf_op jit(solution)/shard_map/pallas_call | solution.py:339
  50.8 1.4 %copy.10 = bf16[8,3072]{1,0:T(8,128)(2,1)} copy(bf16[8,3072]{1,0:T(8,128)(2,1)} %shard_map.82) | data formatting | bytes 98304
